TPU v7x, 32 devices: a whole 2x2x4 slice. The times are simulated.
32 devices in a mesh: groups: 2 (over y), seq: 4 (over z), row: 2 (over x), col: 2 (over core).
Axes of the slice: x: 2, y: 2, z: 4, core: 2. Of those that a mesh axis runs over, the one named last changes fastest.
Arguments:
- acts: bfloat16 [3072, 4096], P(('groups', 'seq', 'row'), 'col'), parts along dimension 0, may hold values from -9 to 9
- w_query: bfloat16 [4096, 2048], P('seq', ('row', 'col')), may hold values from -0.1875 to 0.1875
- w_key: bfloat16 [4096, 2048], P('seq', ('row', 'col')), may hold values from -0.1875 to 0.1875
- w_value: bfloat16 [4096, 2048], P('seq', ('row', 'col')), may hold values from -0.09375 to 0.09375
Outputs:
- attended: bfloat16 [3072, 2048], P(('groups', 'seq'), ('row', 'col')), parts along dimension 0
There are 2 independent parts, one for each index of `groups`. A program takes and returns all parts, laid end to end along the dimension named above; an argument that names none is the same for every part. Nothing has to cross between parts.
All inputs are finite; a program needn't handle non-finite values.
Results may differ from a plain program's by a relative error of at most 0.0055.
The roundings to bfloat16 on the way count: a program that leaves them out, or rounds other values in their place, can miss the bound.
Values may be sent and summed in bfloat16 or wider, within the bound.
A program may use at most 64 MiB of HBM per device.

v0:
```python
import jax
import jax.numpy as jnp
from jax import lax
from jax.sharding import PartitionSpec as P

HD = 128
SPAN = 4


def passed_along(block, axis, distance):
    devices = range(lax.axis_size(axis))
    route = [((i - distance) % len(devices), i) for i in devices]
    return lax.ppermute(block, axis, route)


def per_device(acts, w_query, w_key, w_value):
    block = lax.all_gather(acts, "row", axis=0, tiled=True)
    block = lax.all_gather(block, "col", axis=1, tiled=True)
    tokens_here = block.shape[0]
    width = w_query.shape[1]
    heads_here = width // HD
    pieces = (
        lax.all_gather(w_query, "seq", axis=0, tiled=True),
        lax.all_gather(w_key, "seq", axis=0, tiled=True),
        lax.all_gather(w_value, "seq", axis=0, tiled=True),
    )
    query_sum, key_sum, value_sum = tuple(
        (jnp.dot(block, piece, preferred_element_type=jnp.float32) for piece in pieces)
    )
    query = query_sum.astype(jnp.bfloat16).reshape(tokens_here, heads_here, HD)
    packed = jnp.stack([key_sum.astype(jnp.bfloat16), value_sum.astype(jnp.bfloat16)])
    blocks_seen = [packed]
    current = packed
    for step in range(1, SPAN):
        current = passed_along(current, "seq", 1)
        blocks_seen.append(current)
    scale = 1.0 / jnp.sqrt(jnp.float32(HD))
    score_list = []
    for seen in blocks_seen:
        seen_keys = seen[0].reshape(-1, heads_here, HD)
        score_list.append(
            jnp.einsum("qhd,khd->hqk", query, seen_keys, preferred_element_type=jnp.float32) * scale
        )
    largest = score_list[0].max(axis=-1, keepdims=True)
    for scores in score_list[1:]:
        largest = jnp.maximum(largest, scores.max(axis=-1, keepdims=True))
    running_total = jnp.zeros((heads_here, tokens_here), jnp.float32)
    summed = jnp.zeros((tokens_here, heads_here, HD), jnp.float32)
    for scores, seen in zip(score_list, blocks_seen):
        expos = jnp.exp(scores - largest)
        running_total = running_total + jnp.sum(expos, axis=-1)
        seen_values = seen[1].reshape(-1, heads_here, HD)
        summed = summed + jnp.einsum(
            "hqk,khd->qhd",
            expos.astype(jnp.bfloat16),
            seen_values,
            preferred_element_type=jnp.float32,
        )
    attended = summed / jnp.transpose(running_total)[:, :, None]
    return attended.astype(jnp.bfloat16).reshape(tokens_here, width)


def solution(mesh):
    in_specs = (
        P(("groups", "seq", "row"), "col"),
        P("seq", ("row", "col")),
        P("seq", ("row", "col")),
        P("seq", ("row", "col")),
    )
    out_specs = P(("groups", "seq"), ("row", "col"))
    return jax.shard_map(
        per_device, mesh=mesh, in_specs=in_specs, out_specs=out_specs, check_vma=False
    )
```

profile of v0, /device:TPU:0, one launch (start us, length us, event | category | flops | bytes accessed | tf_op | source)
XLA Modules:
  0.0 381.3 jit_solution(7910305317543473265)
XLA Ops:
  6.5 0.7 all-gather.6.cloned.1.call-update
  7.3 31.5 %all-gather.6.cloned.1.call-done = bf16[384,2048]{1,0:T(8,128)(2,1)} async-done(((bf16[192,2048]{1,0:T(8,128)(2,1)}), bf16[384,2048]{1,0:T(8,128)(2,1)}) %all-gather.6.cloned.1.call-update) | async-done | bytes 1572880 | tf_op jit(solution)/shard_map/all_gather | solution.py:17
  38.9 0.7 all-gather.10.cloned.1.call-update
  40.8 11.8 %all-gather.8.cloned.1.call-done = bf16[384,4096]{1,0:T(8,128)(2,1)} async-done(((bf16[384,2048]{1,0:T(8,128)(2,1)}), bf16[384,4096]{1,0:T(8,128)(2,1)}) %all-gather.8.cloned.1.call-update) | async-done | bytes 3145744 | tf_op jit(solution)/shard_map/all_gather | solution.py:18
  52.5 83.5 %all-gather.10.cloned.1.call-done = bf16[4096,512]{1,0:T(8,128)(2,1)} async-done(((bf16[1024,512]{1,0:T(8,128)(2,1)}), bf16[4096,512]{1,0:T(8,128)(2,1)}) %all-gather.10.cloned.1.call-update) | async-done | bytes 4194320 | tf_op jit(solution)/shard_map/all_gather | solution.py:25
  136.1 4.9 %convolution_convert_fusion.2 = bf16[384,512]{1,0:T(8,128)(2,1)S(1)} fusion(bf16[384,4096]{1,0:T(8,128)(2,1)} %all-gather.8.cloned.1.call-done, bf16[4096,512]{1,0:T(8,128)(2,1)} %all-gather.10.cloned.1.call-done), kind=kOutput, calls=%fused_computation.24 | convolution fusion | flops 1610809344 | bytes 7733248 | tf_op jit(solution)/shard_map/dot_general | solution.py:28
  141.0 75.8 %all-gather.14.cloned.1.call-done = bf16[4096,512]{1,0:T(8,128)(2,1)} async-done(((bf16[1024,512]{1,0:T(8,128)(2,1)}), bf16[4096,512]{1,0:T(8,128)(2,1)}) %all-gather.14.cloned.1.call-update) | async-done | bytes 4194320 | tf_op jit(solution)/shard_map/all_gather | solution.py:24
  216.8 4.9 %convolution_convert_fusion = bf16[384,512]{1,0:T(8,128)(2,1)S(1)} fusion(bf16[384,4096]{1,0:T(8,128)(2,1)} %all-gather.8.cloned.1.call-done, bf16[4096,512]{1,0:T(8,128)(2,1)} %all-gather.14.cloned.1.call-done), kind=kOutput, calls=%fused_computation.22 | convolution fusion | flops 1610809344 | bytes 7733248 | tf_op jit(solution)/shard_map/dot_general | solution.py:28
  221.9 35.7 %collective-permute-done = bf16[2,384,512]{2,1,0:T(8,128)(2,1)} collective-permute-done((bf16[2,384,512]{2,1,0:T(8,128)(2,1)S(1)}, bf16[2,384,512]{2,1,0:T(8,128)(2,1)}, u32[]{:S(2)}, u32[]{:S(2)}) %collective-permute-start) | collective-permute-done | bytes 786464 | tf_op jit(solution)/shard_map/ppermute | solution.py:13
  257.6 10.9 %collective-permute-start.1 = (bf16[2,384,512]{2,1,0:T(8,128)(2,1)}, bf16[2,384,512]{2,1,0:T(8,128)(2,1)}, u32[]{:S(2)}, u32[]{:S(2)}) collective-permute-start(bf16[2,384,512]{2,1,0:T(8,128)(2,1)} %collective-permute-done), channel_id=1, source_target_pairs={{12,0},{0,4},{4,8},{8,12},{13,1},{1,5},{5,9},{9,13},{14,2},{2,6},{... | collective-permute-start | bytes 2359304 | tf_op jit(solution)/shard_map/ppermute | solution.py:13
  268.5 59.4 %all-gather.12.cloned.1.call-done = bf16[4096,512]{1,0:T(8,128)(2,1)} async-done(((bf16[1024,512]{1,0:T(8,128)(2,1)}), bf16[4096,512]{1,0:T(8,128)(2,1)}) %all-gather.12.cloned.1.call-update) | async-done | bytes 4194320 | tf_op jit(solution)/shard_map/all_gather | solution.py:23
  327.9 4.9 %fusion.11 = bf16[48,4,8,128]{3,2,1,0:T(8,128)(2,1)S(1)} fusion(bf16[384,4096]{1,0:T(8,128)(2,1)} %all-gather.8.cloned.1.call-done, bf16[4096,512]{1,0:T(8,128)(2,1)} %all-gather.12.cloned.1.call-done), kind=kOutput, calls=%fused_computation.25 | convolution fusion | flops 1610809344 | bytes 7733248 | tf_op jit(solution)/shard_map/dot_general | solution.py:28
  332.8 0.9 copy.26
  334.2 1.2 fusion.48
  335.4 0.8 reshape_squeeze.18
  336.5 2.9 multiply_reduce_fusion.2
  339.4 1.9 fusion.47
  341.3 0.8 reshape_squeeze.19
  342.1 1.2 copy.28
  343.3 3.5 multiply_reduce_fusion.1
  346.8 11.3 %collective-permute-done.2 = bf16[2,384,512]{2,1,0:T(8,128)(2,1)} collective-permute-done((bf16[2,384,512]{2,1,0:T(8,128)(2,1)}, bf16[2,384,512]{2,1,0:T(8,128)(2,1)}, u32[]{:S(2)}, u32[]{:S(2)}) %collective-permute-start.2) | collective-permute-done | bytes 786464 | tf_op jit(solution)/shard_map/ppermute | solution.py:13
  358.1 2.1 fusion.46
  360.2 1.8 reshape_squeeze.20
  362.0 3.5 multiply_reduce_fusion
  365.5 1.2 copy.29
  366.7 0.9 maximum_maximum_fusion
  367.6 1.7 fusion.15
  369.9 1.1 copy-done.1
  371.0 1.6 fusion.2
  372.6 0.6 convolution_add_fusion.1
  373.2 0.6 fusion.10
  373.9 0.9 copy.21
  (21 shorter events, 2.7 us)
Async XLA Ops:
  6.5 32.3 %all-gather.6.cloned.1.call-start = ((), (), s32[]{:S(2)}) async-start(), calls=%async_computation | async-start | bytes 2359296 | tf_op jit(solution)/shard_map/all_gather | solution.py:17
  7.3 45.3 %all-gather.8.cloned.1.call-start = ((), (), s32[]{:S(2)}) async-start(), calls=%async_computation.1 | async-start | bytes 4718592 | tf_op jit(solution)/shard_map/all_gather | solution.py:18
  38.9 97.2 %all-gather.10.cloned.1.call-start = ((), (), s32[]{:S(2)}) async-start(), calls=%async_computation.2 | async-start | bytes 5242880 | tf_op jit(solution)/shard_map/all_gather | solution.py:25
  39.6 177.2 %all-gather.14.cloned.1.call-start = ((), (), s32[]{:S(2)}) async-start(), calls=%async_computation.4 | async-start | bytes 5242880 | tf_op jit(solution)/shard_map/all_gather | solution.py:24
  40.2 287.7 %all-gather.12.cloned.1.call-start = ((), (), s32[]{:S(2)}) async-start(), calls=%async_computation.3 | async-start | bytes 5242880 | tf_op jit(solution)/shard_map/all_gather | solution.py:23
  221.8 35.7 %collective-permute-start = (bf16[2,384,512]{2,1,0:T(8,128)(2,1)S(1)}, bf16[2,384,512]{2,1,0:T(8,128)(2,1)}, u32[]{:S(2)}, u32[]{:S(2)}) collective-permute-start(bf16[2,384,512]{2,1,0:T(8,128)(2,1)S(1)} %pad_maximum_fusion), channel_id=1, source_target_pairs={{12,0},{0,4},{4,8},{8,12},{13,1},{1,5},{5,9},{9,13},{14,2},{2,6},{... | collective-permute-start | bytes 2359304 | tf_op jit(solution)/shard_map/ppermute | solution.py:13
  257.6 78.8 %collective-permute-start.1 = (bf16[2,384,512]{2,1,0:T(8,128)(2,1)}, bf16[2,384,512]{2,1,0:T(8,128)(2,1)}, u32[]{:S(2)}, u32[]{:S(2)}) collective-permute-start(bf16[2,384,512]{2,1,0:T(8,128)(2,1)} %collective-permute-done), channel_id=1, source_target_pairs={{12,0},{0,4},{4,8},{8,12},{13,1},{1,5},{5,9},{9,13},{14,2},{2,6},{... | collective-permute-start | bytes 2359304 | tf_op jit(solution)/shard_map/ppermute | solution.py:13
  336.4 21.7 %collective-permute-start.2 = (bf16[2,384,512]{2,1,0:T(8,128)(2,1)}, bf16[2,384,512]{2,1,0:T(8,128)(2,1)}, u32[]{:S(2)}, u32[]{:S(2)}) collective-permute-start(bf16[2,384,512]{2,1,0:T(8,128)(2,1)} %collective-permute-done.1), channel_id=1, source_target_pairs={{12,0},{0,4},{4,8},{8,12},{13,1},{1,5},{5,9},{9,13},{14,2},{2,6},{... | collective-permute-start | bytes 2359304 | tf_op jit(solution)/shard_map/ppermute | solution.py:13
  366.7 2.6 copy-start
  367.6 2.3 copy-start.2
  369.3 1.7 copy-start.1
Sparse Core Ops, SparseCore 0:
  8.9 29.8 all-gather.5
  40.4 12.1 all-gather.7
  54.1 81.9 all-gather.9
  137.5 79.2 all-gather.13
  218.2 109.5 all-gather.11
where the time goes:
time: 382 us; the launch traced here: 381 us
  waiting for transfers between devices  311 us (81%)
  matrix products  28.6 us (7%)
  local copies, waits for them, and re-layouts  14.2 us (4%)
  between operations  13.3 us (3%)
  starting transfers between devices  11.2 us (3%)
    all_gather x1, waiting for transfers between devices, per_device(): lax.all_gather(w_value, 'seq', axis=0, tiled=True)  83.5 us
    all_gather x1, waiting for transfers between devices, per_device(): lax.all_gather(w_key, 'seq', axis=0, tiled=True)  75.8 us
    all_gather x1, waiting for transfers between devices, per_device(): lax.all_gather(w_query, 'seq', axis=0, tiled=True)  59.4 us
    ppermute x3, waiting for transfers between devices, passed_along(): return lax.ppermute(block, axis, route)  47 us
    all_gather x1, waiting for transfers between devices, per_device(): block = lax.all_gather(acts, 'row', axis=0, tiled=True)  31.5 us
    dot_general x3, matrix products, per_device(): jnp.dot(block, piece, preferred_element_type=jnp.float32)  14.8 us
    all_gather x1, waiting for transfers between devices, per_device(): block = lax.all_gather(block, 'col', axis=1, tiled=True)  11.8 us
    ppermute x3, starting transfers between devices, passed_along(): return lax.ppermute(block, axis, route)  11 us
  transfers between devices with their start and end apart: 8, of which 7 were waited for; matrix products, arithmetic and copies ran while one was open for 8% of the time, Pallas kernels for 0%

commit v1 on v0

--- a/solution.py
+++ b/solution.py
@@ -1,10 +1,274 @@
+import functools
+
 import jax
 import jax.numpy as jnp
 from jax import lax
+from jax.experimental import pallas as pl
+from jax.experimental.pallas import tpu as pltpu
 from jax.sharding import PartitionSpec as P
 
 HD = 128
 SPAN = 4
+CHUNKS = 4
+MESH = pl.DeviceIdType.MESH
+
+
+def head_kernel(
+    n, acts, w_query, w_key, w_value, out,
+    x_all, w_all, qkv, heads_out,
+    local_sem, w_send, w_recv, y_send, y_recv,
+    up_send, down_send, z_recv, x_send, x_recv, c_send, c_recv, o_send, o_recv,
+):
+    g, s = lax.axis_index("groups"), lax.axis_index("seq")
+    r, c = lax.axis_index("row"), lax.axis_index("col")
+    weights = (w_query, w_key, w_value)
+    rows, half_width = acts.shape
+    depth = w_query.shape[0]
+    half = depth // 2
+    block = 2 * rows
+    part = rows // CHUNKS
+
+    barrier = pltpu.get_barrier_semaphore()
+    for j in range(1, n):
+        pl.semaphore_signal(barrier, inc=1, device_id={"seq": lax.rem(s + j, n)}, device_id_type=MESH)
+    pl.semaphore_signal(barrier, inc=1, device_id={"groups": 1 - g}, device_id_type=MESH)
+    pl.semaphore_signal(barrier, inc=1, device_id={"row": 1 - r}, device_id_type=MESH)
+    pl.semaphore_signal(barrier, inc=1, device_id={"col": 1 - c}, device_id_type=MESH)
+    pl.semaphore_wait(barrier, n + 2)
+
+    def remote(src, dst, send, recv, **device):
+        return pltpu.make_async_remote_copy(
+            src_ref=src, dst_ref=dst, send_sem=send, recv_sem=recv, device_id=device, device_id_type=MESH
+        )
+
+    def w_rows(owner, which):
+        return pl.ds(pl.multiple_of(owner * depth + which * half, half), half)
+
+    def w_copy(j, i):
+        dest = lax.rem(s + j, n)
+        return remote(
+            weights[i].at[pl.ds(pl.multiple_of(g * half, half), half), pl.ds(pl.multiple_of(dest * HD, HD), HD)],
+            w_all.at[w_rows(s, g), pl.ds(i * HD, HD)],
+            w_send.at[j - 1, i], w_recv.at[j - 1, i], seq=dest,
+        )
+
+    def w_arrival(j, i):
+        owner = lax.rem(s + n - j, n)
+        here = w_all.at[w_rows(owner, g), pl.ds(i * HD, HD)]
+        return remote(here, here, w_send.at[j - 1, i], w_recv.at[j - 1, i], seq=lax.rem(s + j, n))
+
+    def y_copy(j):
+        owner = lax.rem(s + n - j, n)
+        here = w_all.at[w_rows(owner, g), :]
+        return remote(here, here, y_send.at[j - 1], y_recv.at[j - 1], groups=1 - g)
+
+    def y_arrival(j):
+        owner = lax.rem(s + n - j, n)
+        here = w_all.at[w_rows(owner, 1 - g), :]
+        return remote(here, here, y_send.at[j - 1], y_recv.at[j - 1], groups=1 - g)
+
+    def spot(b, rr, cc, k):
+        return x_all.at[b, cc, pl.ds(pl.multiple_of(rr * rows + k * part, part), part), :]
+
+    def source(b, k, own):
+        return acts.at[pl.ds(pl.multiple_of(k * part, part), part), :] if own else spot(b, r, c, k)
+
+    def up_copy(b, k, own=False):
+        return remote(source(b, k, own), spot(b, r, c, k), up_send.at[b, k], z_recv.at[b, k], seq=s + 1)
+
+    def down_copy(b, k, own=False):
+        return remote(source(b, k, own), spot(b, r, c, k), down_send.at[b, k], z_recv.at[b, k], seq=s - 1)
+
+    def x_copy(b, k, own=False):
+        return remote(source(b, k, own), spot(b, r, c, k), x_send.at[b, k], x_recv.at[b, k], row=1 - r)
+
+    def x_arrival(b, k):
+        here = spot(b, 1 - r, c, k)
+        return remote(here, here, x_send.at[b, k], x_recv.at[b, k], row=1 - r)
+
+    def c_copy(b, k, rr, own=False):
+        src = source(b, k, True) if own else spot(b, rr, c, k)
+        return remote(src, spot(b, rr, c, k), c_send.at[rr, b, k], c_recv.at[rr, b, k], col=1 - c)
+
+    def c_arrival(b, k, rr):
+        here = spot(b, rr, 1 - c, k)
+        return remote(here, here, c_send.at[rr, b, k], c_recv.at[rr, b, k], col=1 - c)
+
+    for j in range(1, n):
+        for i in range(3):
+            w_copy(j, i).start()
+
+    @pl.loop(0, CHUNKS)
+    def _(k):
+        @pl.when(s < n - 1)
+        def _():
+            up_copy(s, k, True).start()
+
+        @pl.when(s > 0)
+        def _():
+            down_copy(s, k, True).start()
+
+        x_copy(s, k, True).start()
+        c_copy(s, k, r, True).start()
+
+    own_copies = [
+        pltpu.make_async_copy(
+            acts, x_all.at[s, c, pl.ds(pl.multiple_of(r * rows, rows), rows), :], local_sem.at[0]
+        )
+    ] + [
+        pltpu.make_async_copy(
+            weights[i].at[:, pl.ds(pl.multiple_of(s * HD, HD), HD)],
+            w_all.at[pl.ds(pl.multiple_of(s * depth, depth), depth), pl.ds(i * HD, HD)],
+            local_sem.at[1 + i],
+        )
+        for i in range(3)
+    ]
+    for copy in own_copies:
+        copy.start()
+
+    def each_at(t, body):
+        if t == 0:
+            body(s, 0)
+            return
+        pl.when(s - t >= 0)(lambda: body(s - t, 1))
+        pl.when(s + t < n)(lambda: body(s + t, -1))
+
+    def pass_on(b, side, k):
+        here = spot(b, r, c, k)
+        remote(here, here, up_send.at[b, k], z_recv.at[b, k], row=1 - r).wait_recv()
+        if side > 0:
+            pl.when(s < n - 1)(lambda: up_copy(b, k).start())
+        else:
+            pl.when(s > 0)(lambda: down_copy(b, k).start())
+        x_copy(b, k).start()
+        c_copy(b, k, r).start()
+
+    def across(b, k):
+        x_arrival(b, k).wait_recv()
+        c_copy(b, k, 1 - r).start()
+
+    def project(b):
+        @pl.loop(0, CHUNKS)
+        def _(k):
+            c_arrival(b, k, 0).wait_recv()
+            c_arrival(b, k, 1).wait_recv()
+
+        total = jnp.dot(x_all[b, 0], w_all[:half_width, :], preferred_element_type=jnp.float32)
+        total += jnp.dot(x_all[b, 1], w_all[half_width:, :], preferred_element_type=jnp.float32)
+        qkv[pl.ds(pl.multiple_of(b * block, block), block), :] = total.astype(jnp.bfloat16)
+
+    for t in range(1, n):
+        @pl.loop(0, CHUNKS)
+        def _(k):
+            each_at(t, lambda b, side: pass_on(b, side, k))
+            each_at(t - 1, lambda b, side: across(b, k))
+
+        if t == 1:
+            for j in range(1, n):
+                for i in range(3):
+                    w_arrival(j, i).wait_recv()
+                y_copy(j).start()
+        if t == n - 2:
+            for copy in own_copies:
+                copy.wait()
+            for j in range(1, n):
+                y_arrival(j).wait_recv()
+            first, last = jnp.maximum(s - (n - 3), 0), jnp.minimum(s + (n - 3), n - 1)
+            pl.loop(first, last + 1)(project)
+        if t == n - 1:
+            each_at(n - 2, lambda b, side: project(b))
+
+    @pl.loop(0, CHUNKS)
+    def _(k):
+        each_at(n - 1, lambda b, side: across(b, k))
+
+    each_at(n - 1, lambda b, side: project(b))
+
+    scale = 1.0 / jnp.sqrt(jnp.float32(HD))
+
+    def o_copy(j):
+        dest = lax.rem(s + j, n)
+        return remote(
+            heads_out.at[dest], out.at[:, pl.ds(pl.multiple_of(s * HD, HD), HD)],
+            o_send.at[j - 1], o_recv.at[j - 1], seq=dest,
+        )
+
+    def o_arrival(j):
+        owner = lax.rem(s + n - j, n)
+        here = out.at[:, pl.ds(pl.multiple_of(owner * HD, HD), HD)]
+        return remote(heads_out.at[owner], here, o_send.at[j - 1], o_recv.at[j - 1], seq=owner)
+
+    @pl.loop(1, n + 1)
+    def _(j):
+        b = lax.rem(s + j, n)
+        query = qkv[pl.ds(pl.multiple_of(b * block, block), block), pl.ds(0, HD)]
+        keys = qkv[:, pl.ds(HD, HD)]
+        values = qkv[:, pl.ds(2 * HD, HD)]
+        scores = lax.dot_general(
+            query, keys, (((1,), (1,)), ((), ())), preferred_element_type=jnp.float32
+        ) * scale
+        expos = jnp.exp(scores - jnp.max(scores, axis=-1, keepdims=True))
+        total = jnp.sum(expos, axis=-1, keepdims=True)
+        summed = jnp.dot(expos.astype(jnp.bfloat16), values, preferred_element_type=jnp.float32)
+        heads_out[b] = (summed / total).astype(jnp.bfloat16)
+        pl.when(j < n)(lambda: o_copy(j).start())
+
+    own_out = pltpu.make_async_copy(
+        heads_out.at[s], out.at[:, pl.ds(pl.multiple_of(s * HD, HD), HD)], local_sem.at[0]
+    )
+    own_out.start()
+
+    for j in range(1, n):
+        for i in range(3):
+            w_copy(j, i).wait_send()
+        y_copy(j).wait_send()
+
+    @pl.loop(0, n)
+    def _(b):
+        @pl.loop(0, CHUNKS)
+        def _(k):
+            pl.when((s < n - 1) & (b <= s))(lambda: up_copy(b, k).wait_send())
+            pl.when((s > 0) & (b >= s))(lambda: down_copy(b, k).wait_send())
+            x_copy(b, k).wait_send()
+            c_copy(b, k, 0).wait_send()
+            c_copy(b, k, 1).wait_send()
+
+    own_out.wait()
+    for j in range(1, n):
+        o_copy(j).wait_send()
+        o_arrival(j).wait_recv()
+
+
+def one_head_per_device(acts, w_query, w_key, w_value):
+    n = lax.axis_size("seq")
+    rows, half_width = acts.shape
+    depth, width = w_query.shape
+    tokens = n * 2 * rows
+    dma = pltpu.SemaphoreType.DMA
+    anywhere = pl.BlockSpec(memory_space=pl.ANY)
+    flops = 2 * tokens * depth * n * 3 * HD + 4 * tokens * tokens * HD
+    return pl.pallas_call(
+        functools.partial(head_kernel, n),
+        out_shape=jax.ShapeDtypeStruct((2 * rows, width), jnp.bfloat16),
+        in_specs=[anywhere] * 4,
+        out_specs=anywhere,
+        scratch_shapes=[
+            pltpu.VMEM((n, 2, 2 * rows, half_width), jnp.bfloat16),
+            pltpu.VMEM((n * depth, 3 * HD), jnp.bfloat16),
+            pltpu.VMEM((tokens, 3 * HD), jnp.bfloat16),
+            pltpu.VMEM((n, 2 * rows, HD), jnp.bfloat16),
+            dma((4,)),
+            dma((n - 1, 3)), dma((n - 1, 3)), dma((n - 1,)), dma((n - 1,)),
+            dma((n, CHUNKS)), dma((n, CHUNKS)), dma((n, CHUNKS)),
+            dma((n, CHUNKS)), dma((n, CHUNKS)),
+            dma((2, n, CHUNKS)), dma((2, n, CHUNKS)),
+            dma((n - 1,)), dma((n - 1,)),
+        ],
+        compiler_params=pltpu.CompilerParams(
+            collective_id=0, has_side_effects=True, vmem_limit_bytes=48 * 1024 * 1024
+        ),
+        cost_estimate=pl.CostEstimate(flops=flops, bytes_accessed=2 * tokens * half_width, transcendentals=tokens * tokens),
+    )(acts, w_query, w_key, w_value)
 
 
 def passed_along(block, axis, distance):
@@ -13,7 +277,7 @@
     return lax.ppermute(block, axis, route)
 
 
-def per_device(acts, w_query, w_key, w_value):
+def blocks_passed_along(acts, w_query, w_key, w_value):
     block = lax.all_gather(acts, "row", axis=0, tiled=True)
     block = lax.all_gather(block, "col", axis=1, tiled=True)
     tokens_here = block.shape[0]
@@ -60,6 +324,15 @@
     return attended.astype(jnp.bfloat16).reshape(tokens_here, width)
 
 
+def per_device(acts, w_query, w_key, w_value):
+    n = lax.axis_size("seq")
+    pairs = all(lax.axis_size(axis) == 2 for axis in ("groups", "row", "col"))
+    depth, width = w_query.shape
+    if pairs and n == SPAN and width == n * HD and acts.shape[0] % (16 * CHUNKS) == 0 and depth % 32 == 0:
+        return one_head_per_device(acts, w_query, w_key, w_value)
+    return blocks_passed_along(acts, w_query, w_key, w_value)
+
+
 def solution(mesh):
     in_specs = (
         P(("groups", "seq", "row"), "col"),

time: 382 us -> 116 us (0.30)
  waiting for transfers between devices: 311 us -> 0 us
  Pallas kernels: 0 us -> 110 us
  matrix products: 28.6 us -> 0 us
  between operations: 13.3 us -> 0.01 us
  starting transfers between devices: 11.2 us -> 0 us
  local copies, waits for them, and re-layouts: 14.2 us -> 5.55 us
    all_gather x5 -> x0, waiting for transfers between devices: 262 us -> none  [the longest x1 83.5 us: per_device(): lax.all_gather(w_value, 'seq', axis=0, tiled=True)]
    pallas_call x0 -> x1, Pallas kernels: none -> 110 us  [one_head_per_device(): pl.pallas_call(functools.partial(head_kernel, n), out_shape=jax.ShapeDtyp...]
    ppermute x3 -> x0, waiting for transfers between devices: 47 us -> none  [passed_along(): return lax.ppermute(block, axis, route)]
    dot_general x11 -> x0, matrix products: 28.6 us -> none  [the longest x3 14.8 us: per_device(): jnp.dot(block, piece, preferred_element_type=jnp.float32)]
    ppermute x3 -> x0, starting transfers between devices: 11 us -> none  [passed_along(): return lax.ppermute(block, axis, route)]
    another operation x7 -> x0, local copies, waits for them, and re-layouts: 7.03 us -> none  [the longest x4 3.54 us: per_device(): seen_values = seen[1].reshape(-1, heads_here, HD)]
    slice x3 -> x0, local copies, waits for them, and re-layouts: 5.15 us -> none  [per_device(): seen_values = seen[1].reshape(-1, heads_here, HD)]
    unnamed x6 -> x9, local copies, waits for them, and re-layouts: 1.12 us -> 5.55 us
  transfers between devices with their start and end apart: 8 -> 0, of which waited for: 7 -> 0; matrix products, arithmetic and copies ran while one was open for 8% -> 0% of each run, Pallas kernels for 0% -> 0%
where the time goes in v1:
time: 116 us
  Pallas kernels  110 us (95%)
  local copies, waits for them, and re-layouts  5.55 us (5%)
    pallas_call x1, Pallas kernels, one_head_per_device(): pl.pallas_call(functools.partial(head_kernel, n), out_shape=jax.ShapeDtyp...  110 us
    unnamed x9, local copies, waits for them, and re-layouts  5.55 us

profile of v1, /device:TPU:0, one launch (start us, length us, event | category | flops | bytes accessed | tf_op | source)
XLA Modules:
  0.0 115.8 jit_solution(9433660911958940653)
XLA Ops:
  0.0 0.0 copy-start
  0.0 1.2 %copy-done = bf16[1024,512]{1,0:T(8,128)(2,1)S(1)} copy-done((bf16[1024,512]{1,0:T(8,128)(2,1)S(1)}, bf16[1024,512]{1,0:T(8,128)(2,1)}, u32[]{:S(2)}) %copy-start) | copy-done | bytes 1048600
  1.2 0.0 copy-start.1
  1.2 1.2 %copy-done.1 = bf16[1024,512]{1,0:T(8,128)(2,1)S(1)} copy-done((bf16[1024,512]{1,0:T(8,128)(2,1)S(1)}, bf16[1024,512]{1,0:T(8,128)(2,1)}, u32[]{:S(2)}) %copy-start.1) | copy-done | bytes 1048600
  2.5 0.0 copy-start.2
  2.5 1.2 %copy-done.2 = bf16[1024,512]{1,0:T(8,128)(2,1)S(1)} copy-done((bf16[1024,512]{1,0:T(8,128)(2,1)S(1)}, bf16[1024,512]{1,0:T(8,128)(2,1)}, u32[]{:S(2)}) %copy-start.2) | copy-done | bytes 1048600
  3.7 0.0 copy-start.3
  3.7 1.1 copy-done.3
  4.8 110.2 %shard_map.46 = bf16[384,512]{1,0:T(8,128)(2,1)S(1)} custom-call(bf16[192,2048]{1,0:T(8,128)(2,1)S(1)} %copy-done.3, bf16[1024,512]{1,0:T(8,128)(2,1)S(1)} %copy-done, bf16[1024,512]{1,0:T(8,128)(2,1)S(1)} %copy-done.1, bf16[1024,512]{1,0:T(8,128)(2,1)S(1)} %copy-done.2), custom_call_target="tpu_custom_call" | custom-call | flops 6039797760 | bytes 6291456 | tf_op jit(solution)/shard_map/pallas_call | solution.py:250
  115.1 0.7 copy.6
Async XLA Ops:
  0.0 1.2 %copy-start = (bf16[1024,512]{1,0:T(8,128)(2,1)S(1)}, bf16[1024,512]{1,0:T(8,128)(2,1)}, u32[]{:S(2)}) copy-start(bf16[1024,512]{1,0:T(8,128)(2,1)} %w_query.1) | copy-start | bytes 3145732
  1.2 1.2 %copy-start.1 = (bf16[1024,512]{1,0:T(8,128)(2,1)S(1)}, bf16[1024,512]{1,0:T(8,128)(2,1)}, u32[]{:S(2)}) copy-start(bf16[1024,512]{1,0:T(8,128)(2,1)} %w_key.1) | copy-start | bytes 3145732
  2.5 1.2 %copy-start.2 = (bf16[1024,512]{1,0:T(8,128)(2,1)S(1)}, bf16[1024,512]{1,0:T(8,128)(2,1)}, u32[]{:S(2)}) copy-start(bf16[1024,512]{1,0:T(8,128)(2,1)} %w_value.1) | copy-start | bytes 3145732
  3.7 1.1 copy-start.3

commit v2 on v1

--- a/solution.py
+++ b/solution.py
@@ -57,15 +57,13 @@
         here = w_all.at[w_rows(owner, g), pl.ds(i * HD, HD)]
         return remote(here, here, w_send.at[j - 1, i], w_recv.at[j - 1, i], seq=lax.rem(s + j, n))
 
-    def y_copy(j):
+    def y_copy(j, i, which=g):
         owner = lax.rem(s + n - j, n)
-        here = w_all.at[w_rows(owner, g), :]
-        return remote(here, here, y_send.at[j - 1], y_recv.at[j - 1], groups=1 - g)
-
-    def y_arrival(j):
-        owner = lax.rem(s + n - j, n)
-        here = w_all.at[w_rows(owner, 1 - g), :]
-        return remote(here, here, y_send.at[j - 1], y_recv.at[j - 1], groups=1 - g)
+        here = w_all.at[w_rows(owner, which), pl.ds(i * HD, HD)]
+        return remote(here, here, y_send.at[j - 1, i], y_recv.at[j - 1, i], groups=1 - g)
+
+    def y_arrival(j, i):
+        return y_copy(j, i, 1 - g)
 
     def spot(b, rr, cc, k):
         return x_all.at[b, cc, pl.ds(pl.multiple_of(rr * rows + k * part, part), part), :]
@@ -94,8 +92,8 @@
         here = spot(b, rr, 1 - c, k)
         return remote(here, here, c_send.at[rr, b, k], c_recv.at[rr, b, k], col=1 - c)
 
-    for j in range(1, n):
-        for i in range(3):
+    for i in range(3):
+        for j in range(1, n):
             w_copy(j, i).start()
 
     @pl.loop(0, CHUNKS)
@@ -147,42 +145,45 @@
         x_arrival(b, k).wait_recv()
         c_copy(b, k, 1 - r).start()
 
-    def project(b):
-        @pl.loop(0, CHUNKS)
-        def _(k):
-            c_arrival(b, k, 0).wait_recv()
-            c_arrival(b, k, 1).wait_recv()
-
-        total = jnp.dot(x_all[b, 0], w_all[:half_width, :], preferred_element_type=jnp.float32)
-        total += jnp.dot(x_all[b, 1], w_all[half_width:, :], preferred_element_type=jnp.float32)
-        qkv[pl.ds(pl.multiple_of(b * block, block), block), :] = total.astype(jnp.bfloat16)
+    def project(t):
+        @pl.loop(0, 2 if t else 1)
+        def _(side):
+            b = s + (2 * side - 1) * t
+
+            @pl.when((b >= 0) & (b < n))
+            def _():
+                @pl.loop(0, CHUNKS)
+                def _(k):
+                    c_arrival(b, k, 0).wait_recv()
+                    c_arrival(b, k, 1).wait_recv()
+
+                total = jnp.dot(x_all[b, 0], w_all[:half_width, :], preferred_element_type=jnp.float32)
+                total += jnp.dot(x_all[b, 1], w_all[half_width:, :], preferred_element_type=jnp.float32)
+                qkv[pl.ds(pl.multiple_of(b * block, block), block), :] = total.astype(jnp.bfloat16)
 
     for t in range(1, n):
-        @pl.loop(0, CHUNKS)
-        def _(k):
+        for k in range(CHUNKS):
             each_at(t, lambda b, side: pass_on(b, side, k))
             each_at(t - 1, lambda b, side: across(b, k))
-
-        if t == 1:
-            for j in range(1, n):
-                for i in range(3):
-                    w_arrival(j, i).wait_recv()
-                y_copy(j).start()
-        if t == n - 2:
-            for copy in own_copies:
-                copy.wait()
-            for j in range(1, n):
-                y_arrival(j).wait_recv()
-            first, last = jnp.maximum(s - (n - 3), 0), jnp.minimum(s + (n - 3), n - 1)
-            pl.loop(first, last + 1)(project)
-        if t == n - 1:
-            each_at(n - 2, lambda b, side: project(b))
+            if t == 1 and 1 <= k <= 3:
+                for j in range(1, n):
+                    w_arrival(j, k - 1).wait_recv()
+                    y_copy(j, k - 1).start()
+            if t == n - 1 and k == 0:
+                for copy in own_copies:
+                    copy.wait()
+                for j in range(1, n):
+                    for i in range(3):
+                        y_arrival(j, i).wait_recv()
+            if t == n - 1 and k < n - 2:
+                project(k)
+    project(n - 2)
 
     @pl.loop(0, CHUNKS)
     def _(k):
         each_at(n - 1, lambda b, side: across(b, k))
 
-    each_at(n - 1, lambda b, side: project(b))
+    project(n - 1)
 
     scale = 1.0 / jnp.sqrt(jnp.float32(HD))
 
@@ -221,7 +222,7 @@
     for j in range(1, n):
         for i in range(3):
             w_copy(j, i).wait_send()
-        y_copy(j).wait_send()
+            y_copy(j, i).wait_send()
 
     @pl.loop(0, n)
     def _(b):
@@ -245,27 +246,26 @@
     depth, width = w_query.shape
     tokens = n * 2 * rows
     dma = pltpu.SemaphoreType.DMA
-    anywhere = pl.BlockSpec(memory_space=pl.ANY)
     flops = 2 * tokens * depth * n * 3 * HD + 4 * tokens * tokens * HD
     return pl.pallas_call(
         functools.partial(head_kernel, n),
         out_shape=jax.ShapeDtypeStruct((2 * rows, width), jnp.bfloat16),
-        in_specs=[anywhere] * 4,
-        out_specs=anywhere,
+        in_specs=[pl.BlockSpec(memory_space=pl.ANY)] * 4,
+        out_specs=pl.BlockSpec(memory_space=pl.ANY),
         scratch_shapes=[
             pltpu.VMEM((n, 2, 2 * rows, half_width), jnp.bfloat16),
             pltpu.VMEM((n * depth, 3 * HD), jnp.bfloat16),
             pltpu.VMEM((tokens, 3 * HD), jnp.bfloat16),
             pltpu.VMEM((n, 2 * rows, HD), jnp.bfloat16),
             dma((4,)),
-            dma((n - 1, 3)), dma((n - 1, 3)), dma((n - 1,)), dma((n - 1,)),
+            dma((n - 1, 3)), dma((n - 1, 3)), dma((n - 1, 3)), dma((n - 1, 3)),
             dma((n, CHUNKS)), dma((n, CHUNKS)), dma((n, CHUNKS)),
             dma((n, CHUNKS)), dma((n, CHUNKS)),
             dma((2, n, CHUNKS)), dma((2, n, CHUNKS)),
             dma((n - 1,)), dma((n - 1,)),
         ],
         compiler_params=pltpu.CompilerParams(
-            collective_id=0, has_side_effects=True, vmem_limit_bytes=48 * 1024 * 1024
+            collective_id=0, has_side_effects=True, vmem_limit_bytes=63 * 1024 * 1024
         ),
         cost_estimate=pl.CostEstimate(flops=flops, bytes_accessed=2 * tokens * half_width, transcendentals=tokens * tokens),
     )(acts, w_query, w_key, w_value)

time: 116 us -> 110 us (0.948)
  local copies, waits for them, and re-layouts: 5.55 us -> 1.77 us
  Pallas kernels: 110 us -> 108 us
    unnamed x9 -> x1, local copies, waits for them, and re-layouts: 5.55 us -> 1.77 us
    pallas_call x1, Pallas kernels: 110 us -> 108 us  [one_head_per_device(): pl.pallas_call(functools.partial(head_kernel, n), out_shape=jax.ShapeDtyp...]
where the time goes in v2:
time: 110 us
  Pallas kernels  108 us (98%)
  local copies, waits for them, and re-layouts  1.77 us (2%)
    pallas_call x1, Pallas kernels, one_head_per_device(): pl.pallas_call(functools.partial(head_kernel, n), out_shape=jax.ShapeDtyp...  108 us

profile of v2, /device:TPU:0, one launch (start us, length us, event | category | flops | bytes accessed | tf_op | source)
XLA Modules:
  0.0 109.6 jit_solution(4332220243488658506)
XLA Ops:
  0.0 107.8 %shard_map.46 = bf16[384,512]{1,0:T(8,128)(2,1)} custom-call(bf16[192,2048]{1,0:T(8,128)(2,1)} %acts.1, bf16[1024,512]{1,0:T(8,128)(2,1)} %w_query.1, bf16[1024,512]{1,0:T(8,128)(2,1)} %w_key.1, bf16[1024,512]{1,0:T(8,128)(2,1)} %w_value.1), custom_call_target="tpu_custom_call" | custom-call | flops 6039797760 | bytes 6291456 | tf_op jit(solution)/shard_map/pallas_call | solution.py:250
  107.8 1.8 %copy.6 = bf16[384,512]{1,0:T(8,128)(2,1)} copy(bf16[384,512]{1,0:T(8,128)(2,1)} %shard_map.46) | data formatting | bytes 786432

commit v3 on v2

--- a/solution.py
+++ b/solution.py
@@ -1,4 +1,5 @@
 import functools
+import math
 
 import jax
 import jax.numpy as jnp
@@ -9,7 +10,7 @@
 
 HD = 128
 SPAN = 4
-CHUNKS = 4
+CHUNKS = 6
 MESH = pl.DeviceIdType.MESH
 
 
@@ -185,7 +186,7 @@
 
     project(n - 1)
 
-    scale = 1.0 / jnp.sqrt(jnp.float32(HD))
+    rate = math.log2(math.e) / math.sqrt(HD)
 
     def o_copy(j):
         dest = lax.rem(s + j, n)
@@ -207,8 +208,8 @@
         values = qkv[:, pl.ds(2 * HD, HD)]
         scores = lax.dot_general(
             query, keys, (((1,), (1,)), ((), ())), preferred_element_type=jnp.float32
-        ) * scale
-        expos = jnp.exp(scores - jnp.max(scores, axis=-1, keepdims=True))
+        )
+        expos = jnp.exp2((scores - jnp.max(scores, axis=-1, keepdims=True)) * rate)
         total = jnp.sum(expos, axis=-1, keepdims=True)
         summed = jnp.dot(expos.astype(jnp.bfloat16), values, preferred_element_type=jnp.float32)
         heads_out[b] = (summed / total).astype(jnp.bfloat16)

time: 110 us -> 109 us (level)
  no operation moved by 1% of the time
where the time goes in v3:
time: 109 us
  Pallas kernels  107 us (98%)
  local copies, waits for them, and re-layouts  1.77 us (2%)
    pallas_call x1, Pallas kernels, one_head_per_device(): pl.pallas_call(functools.partial(head_kernel, n), out_shape=jax.ShapeDtyp...  107 us

profile of v3, /device:TPU:0, one launch (start us, length us, event | category | flops | bytes accessed | tf_op | source)
XLA Modules:
  0.0 108.8 jit_solution(8818532277460838033)
XLA Ops:
  0.0 107.0 %shard_map.46 = bf16[384,512]{1,0:T(8,128)(2,1)} custom-call(bf16[192,2048]{1,0:T(8,128)(2,1)} %acts.1, bf16[1024,512]{1,0:T(8,128)(2,1)} %w_query.1, bf16[1024,512]{1,0:T(8,128)(2,1)} %w_key.1, bf16[1024,512]{1,0:T(8,128)(2,1)} %w_value.1), custom_call_target="tpu_custom_call" | custom-call | flops 6039797760 | bytes 6291456 | tf_op jit(solution)/shard_map/pallas_call | solution.py:251
  107.0 1.8 %copy.6 = bf16[384,512]{1,0:T(8,128)(2,1)} copy(bf16[384,512]{1,0:T(8,128)(2,1)} %shard_map.46) | data formatting | bytes 786432

commit v4 on v3

--- a/solution.py
+++ b/solution.py
@@ -16,7 +16,7 @@
 
 def head_kernel(
     n, acts, w_query, w_key, w_value, out,
-    x_all, w_all, qkv, heads_out,
+    x_all, w_all, qkv, heads_out, tops, totals, sums,
     local_sem, w_send, w_recv, y_send, y_recv,
     up_send, down_send, z_recv, x_send, x_recv, c_send, c_recv, o_send, o_recv,
 ):
@@ -162,7 +162,32 @@
                 total += jnp.dot(x_all[b, 1], w_all[half_width:, :], preferred_element_type=jnp.float32)
                 qkv[pl.ds(pl.multiple_of(b * block, block), block), :] = total.astype(jnp.bfloat16)
 
-    for t in range(1, n):
+    rate = math.log2(math.e) / math.sqrt(HD)
+    at_end = (s == 0) | (s == n - 1)
+    far = n - 1 - s
+
+    def of_block(b, what):
+        return qkv[pl.ds(pl.multiple_of(b * block, block), block), pl.ds(what * HD, HD)]
+
+    def scores_of(query, keys):
+        return lax.dot_general(query, keys, (((1,), (1,)), ((), ())), preferred_element_type=jnp.float32)
+
+    def weigh(scores, top, values):
+        expos = jnp.exp2((scores - top) * rate)
+        summed = jnp.dot(expos.astype(jnp.bfloat16), values, preferred_element_type=jnp.float32)
+        return jnp.sum(expos, axis=-1, keepdims=True), summed
+
+    def attend_near(i):
+        @pl.when(at_end)
+        def _():
+            b = jnp.where(s == 0, i, n - 1 - i)
+            near = pl.ds(pl.multiple_of(jnp.where(s == 0, 0, block), block), (n - 1) * block)
+            scores = scores_of(of_block(b, 0), qkv[near, pl.ds(HD, HD)])
+            top = jnp.max(scores, axis=-1, keepdims=True)
+            tops[b] = top
+            totals[b], sums[b] = weigh(scores, top, qkv[near, pl.ds(2 * HD, HD)])
+
+    for t in range(1, n - 1):
         for k in range(CHUNKS):
             each_at(t, lambda b, side: pass_on(b, side, k))
             each_at(t - 1, lambda b, side: across(b, k))
@@ -170,15 +195,25 @@
                 for j in range(1, n):
                     w_arrival(j, k - 1).wait_recv()
                     y_copy(j, k - 1).start()
-            if t == n - 1 and k == 0:
-                for copy in own_copies:
-                    copy.wait()
-                for j in range(1, n):
-                    for i in range(3):
-                        y_arrival(j, i).wait_recv()
-            if t == n - 1 and k < n - 2:
-                project(k)
-    project(n - 2)
+
+    for k in range(CHUNKS):
+        each_at(n - 1, lambda b, side: pass_on(b, side, k))
+        if k == 0:
+            for copy in own_copies:
+                copy.wait()
+            for j in range(1, n):
+                for i in range(3):
+                    y_arrival(j, i).wait_recv()
+        if k < 2:
+            @pl.loop(k * (CHUNKS // 2), (k + 1) * (CHUNKS // 2))
+            def _(kk):
+                each_at(n - 2, lambda b, side: across(b, kk))
+        if k < n - 1:
+            project(k)
+        if k == 3:
+            pl.loop(0, 2)(attend_near)
+        if k == 4:
+            attend_near(2)
 
     @pl.loop(0, CHUNKS)
     def _(k):
@@ -186,13 +221,11 @@
 
     project(n - 1)
 
-    rate = math.log2(math.e) / math.sqrt(HD)
-
-    def o_copy(j):
-        dest = lax.rem(s + j, n)
+    def o_copy(b):
+        j = lax.rem(b - s + n, n)
         return remote(
-            heads_out.at[dest], out.at[:, pl.ds(pl.multiple_of(s * HD, HD), HD)],
-            o_send.at[j - 1], o_recv.at[j - 1], seq=dest,
+            heads_out.at[b], out.at[:, pl.ds(pl.multiple_of(s * HD, HD), HD)],
+            o_send.at[j - 1], o_recv.at[j - 1], seq=b,
         )
 
     def o_arrival(j):
@@ -200,20 +233,28 @@
         here = out.at[:, pl.ds(pl.multiple_of(owner * HD, HD), HD)]
         return remote(heads_out.at[owner], here, o_send.at[j - 1], o_recv.at[j - 1], seq=owner)
 
-    @pl.loop(1, n + 1)
+    def give(b, summed, total):
+        heads_out[b] = (summed / total).astype(jnp.bfloat16)
+        pl.when(b != s)(lambda: o_copy(b).start())
+
+    @pl.loop(1, jnp.where(at_end, 2, n + 1))
     def _(j):
-        b = lax.rem(s + j, n)
-        query = qkv[pl.ds(pl.multiple_of(b * block, block), block), pl.ds(0, HD)]
-        keys = qkv[:, pl.ds(HD, HD)]
-        values = qkv[:, pl.ds(2 * HD, HD)]
-        scores = lax.dot_general(
-            query, keys, (((1,), (1,)), ((), ())), preferred_element_type=jnp.float32
-        )
-        expos = jnp.exp2((scores - jnp.max(scores, axis=-1, keepdims=True)) * rate)
-        total = jnp.sum(expos, axis=-1, keepdims=True)
-        summed = jnp.dot(expos.astype(jnp.bfloat16), values, preferred_element_type=jnp.float32)
-        heads_out[b] = (summed / total).astype(jnp.bfloat16)
-        pl.when(j < n)(lambda: o_copy(j).start())
+        b = jnp.where(at_end, far, lax.rem(s + j, n))
+        scores = scores_of(of_block(b, 0), qkv[:, pl.ds(HD, HD)])
+        top = jnp.max(scores, axis=-1, keepdims=True)
+        total, summed = weigh(scores, top, qkv[:, pl.ds(2 * HD, HD)])
+        give(b, summed, total)
+
+    @pl.when(at_end)
+    def _():
+        @pl.loop(0, n - 1)
+        def _(i):
+            b = jnp.where(s == 0, n - 2 - i, 1 + i)
+            scores = scores_of(of_block(b, 0), of_block(far, 1))
+            top = jnp.maximum(tops[b], jnp.max(scores, axis=-1, keepdims=True))
+            total, summed = weigh(scores, top, of_block(far, 2))
+            shrink = jnp.exp2((tops[b] - top) * rate)
+            give(b, sums[b] * shrink + summed, totals[b] * shrink + total)
 
     own_out = pltpu.make_async_copy(
         heads_out.at[s], out.at[:, pl.ds(pl.multiple_of(s * HD, HD), HD)], local_sem.at[0]
@@ -237,7 +278,7 @@
 
     own_out.wait()
     for j in range(1, n):
-        o_copy(j).wait_send()
+        o_copy(lax.rem(s + j, n)).wait_send()
         o_arrival(j).wait_recv()
 
 
@@ -258,6 +299,9 @@
             pltpu.VMEM((n * depth, 3 * HD), jnp.bfloat16),
             pltpu.VMEM((tokens, 3 * HD), jnp.bfloat16),
             pltpu.VMEM((n, 2 * rows, HD), jnp.bfloat16),
+            pltpu.VMEM((n, 2 * rows, 1), jnp.float32),
+            pltpu.VMEM((n, 2 * rows, 1), jnp.float32),
+            pltpu.VMEM((n, 2 * rows, HD), jnp.float32),
             dma((4,)),
             dma((n - 1, 3)), dma((n - 1, 3)), dma((n - 1, 3)), dma((n - 1, 3)),
             dma((n, CHUNKS)), dma((n, CHUNKS)), dma((n, CHUNKS)),

time: 109 us -> 112 us (1.028)
  Pallas kernels: 107 us -> 110 us
    pallas_call x1, Pallas kernels: 107 us -> 110 us  [one_head_per_device(): pl.pallas_call(functools.partial(head_kernel, n), out_shape=jax.ShapeDtyp...]
where the time goes in v4:
time: 112 us
  Pallas kernels  110 us (98%)
  local copies, waits for them, and re-layouts  1.77 us (2%)
    pallas_call x1, Pallas kernels, one_head_per_device(): pl.pallas_call(functools.partial(head_kernel, n), out_shape=jax.ShapeDtyp...  110 us

profile of v4, /device:TPU:0, one launch (start us, length us, event | category | flops | bytes accessed | tf_op | source)
XLA Modules:
  0.0 112.2 jit_solution(6660945516465727793)
XLA Ops:
  0.0 110.4 %shard_map.46 = bf16[384,512]{1,0:T(8,128)(2,1)} custom-call(bf16[192,2048]{1,0:T(8,128)(2,1)} %acts.1, bf16[1024,512]{1,0:T(8,128)(2,1)} %w_query.1, bf16[1024,512]{1,0:T(8,128)(2,1)} %w_key.1, bf16[1024,512]{1,0:T(8,128)(2,1)} %w_value.1), custom_call_target="tpu_custom_call" | custom-call | flops 6039797760 | bytes 6291456 | tf_op jit(solution)/shard_map/pallas_call | solution.py:292
  110.4 1.8 %copy.6 = bf16[384,512]{1,0:T(8,128)(2,1)} copy(bf16[384,512]{1,0:T(8,128)(2,1)} %shard_map.46) | data formatting | bytes 786432

commit v5 on v3

--- a/solution.py
+++ b/solution.py
@@ -16,9 +16,9 @@
 
 def head_kernel(
     n, acts, w_query, w_key, w_value, out,
-    x_all, w_all, qkv, heads_out,
-    local_sem, w_send, w_recv, y_send, y_recv,
-    up_send, down_send, z_recv, x_send, x_recv, c_send, c_recv, o_send, o_recv,
+    x_all, w_all, given, qkv, heads_out,
+    local_sem, w_send, w_recv, y_send, y_recv, xw_send, xw_recv,
+    up_send, down_send, z_recv, c_send, c_recv, q_send, q_recv, o_send, o_recv,
 ):
     g, s = lax.axis_index("groups"), lax.axis_index("seq")
     r, c = lax.axis_index("row"), lax.axis_index("col")
@@ -26,8 +26,8 @@
     rows, half_width = acts.shape
     depth = w_query.shape[0]
     half = depth // 2
-    block = 2 * rows
     part = rows // CHUNKS
+    mine, other = pl.ds(0, 3 * HD), pl.ds(3 * HD, 3 * HD)
 
     barrier = pltpu.get_barrier_semaphore()
     for j in range(1, n):
@@ -42,149 +42,150 @@
             src_ref=src, dst_ref=dst, send_sem=send, recv_sem=recv, device_id=device, device_id_type=MESH
         )
 
-    def w_rows(owner, which):
+    def w_rows(j, which):
+        owner = lax.rem(s + n - j, n)
         return pl.ds(pl.multiple_of(owner * depth + which * half, half), half)
 
     def w_copy(j, i):
         dest = lax.rem(s + j, n)
         return remote(
             weights[i].at[pl.ds(pl.multiple_of(g * half, half), half), pl.ds(pl.multiple_of(dest * HD, HD), HD)],
-            w_all.at[w_rows(s, g), pl.ds(i * HD, HD)],
+            w_all.at[w_rows(0, g), pl.ds(i * HD, HD)],
             w_send.at[j - 1, i], w_recv.at[j - 1, i], seq=dest,
         )
 
     def w_arrival(j, i):
-        owner = lax.rem(s + n - j, n)
-        here = w_all.at[w_rows(owner, g), pl.ds(i * HD, HD)]
+        here = w_all.at[w_rows(j, g), pl.ds(i * HD, HD)]
         return remote(here, here, w_send.at[j - 1, i], w_recv.at[j - 1, i], seq=lax.rem(s + j, n))
 
-    def y_copy(j, i, which=g):
-        owner = lax.rem(s + n - j, n)
-        here = w_all.at[w_rows(owner, which), pl.ds(i * HD, HD)]
-        return remote(here, here, y_send.at[j - 1, i], y_recv.at[j - 1, i], groups=1 - g)
-
-    def y_arrival(j, i):
-        return y_copy(j, i, 1 - g)
-
-    def spot(b, rr, cc, k):
-        return x_all.at[b, cc, pl.ds(pl.multiple_of(rr * rows + k * part, part), part), :]
+    def y_copy(j, whose, which=g):
+        here = w_all.at[w_rows(j, which), (mine, other)[whose]]
+        return remote(here, here, y_send.at[j - 1, whose], y_recv.at[j - 1, whose], groups=1 - g)
+
+    def y_arrival(j, whose):
+        return y_copy(j, whose, 1 - g)
+
+    def xw_copy(j):
+        span = w_rows(j, g) if j else pl.ds(pl.multiple_of(s * depth, depth), depth)
+        return remote(w_all.at[span, mine], w_all.at[span, other], xw_send.at[j], xw_recv.at[j], row=1 - r)
+
+    def xw_arrival(j):
+        span = w_rows(j, g) if j else pl.ds(pl.multiple_of(s * depth, depth), depth)
+        here = w_all.at[span, other]
+        return remote(here, here, xw_send.at[j], xw_recv.at[j], row=1 - r)
+
+    def spot(b, cc, k):
+        return x_all.at[cc, pl.ds(pl.multiple_of(b * rows + k * part, part), part), :]
 
     def source(b, k, own):
-        return acts.at[pl.ds(pl.multiple_of(k * part, part), part), :] if own else spot(b, r, c, k)
+        return acts.at[pl.ds(pl.multiple_of(k * part, part), part), :] if own else spot(b, c, k)
 
     def up_copy(b, k, own=False):
-        return remote(source(b, k, own), spot(b, r, c, k), up_send.at[b, k], z_recv.at[b, k], seq=s + 1)
+        return remote(source(b, k, own), spot(b, c, k), up_send.at[b, k], z_recv.at[b, k], seq=s + 1)
 
     def down_copy(b, k, own=False):
-        return remote(source(b, k, own), spot(b, r, c, k), down_send.at[b, k], z_recv.at[b, k], seq=s - 1)
-
-    def x_copy(b, k, own=False):
-        return remote(source(b, k, own), spot(b, r, c, k), x_send.at[b, k], x_recv.at[b, k], row=1 - r)
-
-    def x_arrival(b, k):
-        here = spot(b, 1 - r, c, k)
-        return remote(here, here, x_send.at[b, k], x_recv.at[b, k], row=1 - r)
-
-    def c_copy(b, k, rr, own=False):
-        src = source(b, k, True) if own else spot(b, rr, c, k)
-        return remote(src, spot(b, rr, c, k), c_send.at[rr, b, k], c_recv.at[rr, b, k], col=1 - c)
-
-    def c_arrival(b, k, rr):
-        here = spot(b, rr, 1 - c, k)
-        return remote(here, here, c_send.at[rr, b, k], c_recv.at[rr, b, k], col=1 - c)
-
-    for i in range(3):
-        for j in range(1, n):
-            w_copy(j, i).start()
-
-    @pl.loop(0, CHUNKS)
-    def _(k):
-        @pl.when(s < n - 1)
-        def _():
-            up_copy(s, k, True).start()
-
-        @pl.when(s > 0)
-        def _():
-            down_copy(s, k, True).start()
-
-        x_copy(s, k, True).start()
-        c_copy(s, k, r, True).start()
+        return remote(source(b, k, own), spot(b, c, k), down_send.at[b, k], z_recv.at[b, k], seq=s - 1)
+
+    def c_copy(b, k, own=False):
+        return remote(source(b, k, own), spot(b, c, k), c_send.at[b, k], c_recv.at[b, k], col=1 - c)
+
+    def c_arrival(b, k):
+        here = spot(b, 1 - c, k)
+        return remote(here, here, c_send.at[b, k], c_recv.at[b, k], col=1 - c)
 
     own_copies = [
-        pltpu.make_async_copy(
-            acts, x_all.at[s, c, pl.ds(pl.multiple_of(r * rows, rows), rows), :], local_sem.at[0]
-        )
-    ] + [
         pltpu.make_async_copy(
             weights[i].at[:, pl.ds(pl.multiple_of(s * HD, HD), HD)],
             w_all.at[pl.ds(pl.multiple_of(s * depth, depth), depth), pl.ds(i * HD, HD)],
-            local_sem.at[1 + i],
+            local_sem.at[i],
         )
         for i in range(3)
     ]
     for copy in own_copies:
         copy.start()
+    for i in range(3):
+        for j in range(1, n):
+            w_copy(j, i).start()
+
+    @pl.loop(0, CHUNKS)
+    def _(k):
+        pl.when(s < n - 1)(lambda: up_copy(s, k, True).start())
+        pl.when(s > 0)(lambda: down_copy(s, k, True).start())
+        c_copy(s, k, True).start()
+
+    own_acts = pltpu.make_async_copy(
+        acts, x_all.at[c, pl.ds(pl.multiple_of(s * rows, rows), rows), :], local_sem.at[3]
+    )
+    own_acts.start()
+    for copy in own_copies:
+        copy.wait()
+    xw_copy(0).start()
 
     def each_at(t, body):
-        if t == 0:
-            body(s, 0)
-            return
         pl.when(s - t >= 0)(lambda: body(s - t, 1))
         pl.when(s + t < n)(lambda: body(s + t, -1))
 
     def pass_on(b, side, k):
-        here = spot(b, r, c, k)
-        remote(here, here, up_send.at[b, k], z_recv.at[b, k], row=1 - r).wait_recv()
+        here = spot(b, c, k)
+        remote(here, here, up_send.at[b, k], z_recv.at[b, k], col=1 - c).wait_recv()
         if side > 0:
             pl.when(s < n - 1)(lambda: up_copy(b, k).start())
         else:
             pl.when(s > 0)(lambda: down_copy(b, k).start())
-        x_copy(b, k).start()
-        c_copy(b, k, r).start()
-
-    def across(b, k):
-        x_arrival(b, k).wait_recv()
-        c_copy(b, k, 1 - r).start()
-
-    def project(t):
-        @pl.loop(0, 2 if t else 1)
-        def _(side):
-            b = s + (2 * side - 1) * t
-
-            @pl.when((b >= 0) & (b < n))
-            def _():
-                @pl.loop(0, CHUNKS)
-                def _(k):
-                    c_arrival(b, k, 0).wait_recv()
-                    c_arrival(b, k, 1).wait_recv()
-
-                total = jnp.dot(x_all[b, 0], w_all[:half_width, :], preferred_element_type=jnp.float32)
-                total += jnp.dot(x_all[b, 1], w_all[half_width:, :], preferred_element_type=jnp.float32)
-                qkv[pl.ds(pl.multiple_of(b * block, block), block), :] = total.astype(jnp.bfloat16)
+        c_copy(b, k).start()
+
+    low = s < n // 2
+    near = pl.multiple_of(jnp.where(low, 0, rows), rows)
+    far = pl.multiple_of(jnp.where(low, (n - 1) * rows, 0), rows)
+    home = pl.multiple_of(r * n * rows, rows)
+
+    def q_copy(start, size, which):
+        return remote(
+            given.at[pl.ds(start, size), :], qkv.at[pl.ds(pl.multiple_of(home + start, rows), size), :],
+            q_send.at[which], q_recv.at[which], row=1 - r,
+        )
+
+    def q_arrival(start, size, which):
+        there = pl.multiple_of((1 - r) * n * rows + start, rows)
+        return remote(
+            given.at[pl.ds(start, size), :], qkv.at[pl.ds(there, size), :], q_send.at[which], q_recv.at[which], row=1 - r
+        )
+
+    def project(start, size, which):
+        @pl.loop(0, size // rows)
+        def _(i):
+            @pl.loop(0, CHUNKS)
+            def _(k):
+                c_arrival(start // rows + i, k).wait_recv()
+
+        span = pl.ds(start, size)
+        total = jnp.dot(x_all[0, span, :], w_all[:half_width, :], preferred_element_type=jnp.float32)
+        total += jnp.dot(x_all[1, span, :], w_all[half_width:, :], preferred_element_type=jnp.float32)
+        given[span, :] = total[:, 3 * HD:].astype(jnp.bfloat16)
+        q_copy(start, size, which).start()
+        qkv[pl.ds(pl.multiple_of(home + start, rows), size), :] = total[:, :3 * HD].astype(jnp.bfloat16)
 
     for t in range(1, n):
         for k in range(CHUNKS):
             each_at(t, lambda b, side: pass_on(b, side, k))
-            each_at(t - 1, lambda b, side: across(b, k))
-            if t == 1 and 1 <= k <= 3:
+            if t == 1 and 1 <= k < n:
+                for i in range(3):
+                    w_arrival(k, i).wait_recv()
+                y_copy(k, 0).start()
+                xw_copy(k).start()
+            if t == 2 and 1 <= k < n:
+                xw_arrival(k).wait_recv()
+                y_copy(k, 1).start()
+            if t == n - 1 and k == CHUNKS - 2:
+                own_acts.wait()
+                xw_arrival(0).wait_recv()
                 for j in range(1, n):
-                    w_arrival(j, k - 1).wait_recv()
-                    y_copy(j, k - 1).start()
-            if t == n - 1 and k == 0:
-                for copy in own_copies:
-                    copy.wait()
-                for j in range(1, n):
-                    for i in range(3):
-                        y_arrival(j, i).wait_recv()
-            if t == n - 1 and k < n - 2:
-                project(k)
-    project(n - 2)
-
-    @pl.loop(0, CHUNKS)
-    def _(k):
-        each_at(n - 1, lambda b, side: across(b, k))
-
-    project(n - 1)
+                    y_arrival(j, 0).wait_recv()
+                    y_arrival(j, 1).wait_recv()
+                project(near, (n - 1) * rows, 0)
+    project(far, rows, 1)
+    q_arrival(near, (n - 1) * rows, 0).wait_recv()
+    q_arrival(far, rows, 1).wait_recv()
 
     rate = math.log2(math.e) / math.sqrt(HD)
 
@@ -203,7 +204,9 @@
     @pl.loop(1, n + 1)
     def _(j):
         b = lax.rem(s + j, n)
-        query = qkv[pl.ds(pl.multiple_of(b * block, block), block), pl.ds(0, HD)]
+        query = jnp.concatenate([
+            qkv[pl.ds(pl.multiple_of((rr * n + b) * rows, rows), rows), pl.ds(0, HD)] for rr in range(2)
+        ])
         keys = qkv[:, pl.ds(HD, HD)]
         values = qkv[:, pl.ds(2 * HD, HD)]
         scores = lax.dot_general(
@@ -220,10 +223,13 @@
     )
     own_out.start()
 
+    xw_copy(0).wait_send()
     for j in range(1, n):
         for i in range(3):
             w_copy(j, i).wait_send()
-            y_copy(j, i).wait_send()
+        y_copy(j, 0).wait_send()
+        y_copy(j, 1).wait_send()
+        xw_copy(j).wait_send()
 
     @pl.loop(0, n)
     def _(b):
@@ -231,10 +237,10 @@
         def _(k):
             pl.when((s < n - 1) & (b <= s))(lambda: up_copy(b, k).wait_send())
             pl.when((s > 0) & (b >= s))(lambda: down_copy(b, k).wait_send())
-            x_copy(b, k).wait_send()
-            c_copy(b, k, 0).wait_send()
-            c_copy(b, k, 1).wait_send()
-
+            c_copy(b, k).wait_send()
+
+    q_copy(near, (n - 1) * rows, 0).wait_send()
+    q_copy(far, rows, 1).wait_send()
     own_out.wait()
     for j in range(1, n):
         o_copy(j).wait_send()
@@ -247,22 +253,23 @@
     depth, width = w_query.shape
     tokens = n * 2 * rows
     dma = pltpu.SemaphoreType.DMA
+    anywhere = pl.BlockSpec(memory_space=pl.ANY)
     flops = 2 * tokens * depth * n * 3 * HD + 4 * tokens * tokens * HD
     return pl.pallas_call(
         functools.partial(head_kernel, n),
         out_shape=jax.ShapeDtypeStruct((2 * rows, width), jnp.bfloat16),
-        in_specs=[pl.BlockSpec(memory_space=pl.ANY)] * 4,
-        out_specs=pl.BlockSpec(memory_space=pl.ANY),
+        in_specs=[anywhere] * 4,
+        out_specs=anywhere,
         scratch_shapes=[
-            pltpu.VMEM((n, 2, 2 * rows, half_width), jnp.bfloat16),
-            pltpu.VMEM((n * depth, 3 * HD), jnp.bfloat16),
+            pltpu.VMEM((2, n * rows, half_width), jnp.bfloat16),
+            pltpu.VMEM((n * depth, 6 * HD), jnp.bfloat16),
+            pltpu.VMEM((n * rows, 3 * HD), jnp.bfloat16),
             pltpu.VMEM((tokens, 3 * HD), jnp.bfloat16),
             pltpu.VMEM((n, 2 * rows, HD), jnp.bfloat16),
             dma((4,)),
-            dma((n - 1, 3)), dma((n - 1, 3)), dma((n - 1, 3)), dma((n - 1, 3)),
-            dma((n, CHUNKS)), dma((n, CHUNKS)), dma((n, CHUNKS)),
-            dma((n, CHUNKS)), dma((n, CHUNKS)),
-            dma((2, n, CHUNKS)), dma((2, n, CHUNKS)),
+            dma((n - 1, 3)), dma((n - 1, 3)), dma((n - 1, 2)), dma((n - 1, 2)), dma((n,)), dma((n,)),
+            dma((n, CHUNKS)), dma((n, CHUNKS)), dma((n, CHUNKS)), dma((n, CHUNKS)), dma((n, CHUNKS)),
+            dma((2,)), dma((2,)),
             dma((n - 1,)), dma((n - 1,)),
         ],
         compiler_params=pltpu.CompilerParams(

time: 109 us -> 129 us (1.18)
  Pallas kernels: 107 us -> 127 us
    pallas_call x1, Pallas kernels: 107 us -> 127 us  [one_head_per_device(): pl.pallas_call(functools.partial(head_kernel, n), out_shape=jax.ShapeDtyp...]
where the time goes in v5:
time: 129 us; the launch traced here: 128 us
  Pallas kernels  127 us (98%)
  local copies, waits for them, and re-layouts  1.77 us (1%)
    pallas_call x1, Pallas kernels, one_head_per_device(): pl.pallas_call(functools.partial(head_kernel, n), out_shape=jax.ShapeDtyp...  127 us

profile of v5, /device:TPU:0, one launch (start us, length us, event | category | flops | bytes accessed | tf_op | source)
XLA Modules:
  0.0 128.5 jit_solution(1126903802253444181)
XLA Ops:
  0.0 126.7 %shard_map.46 = bf16[384,512]{1,0:T(8,128)(2,1)} custom-call(bf16[192,2048]{1,0:T(8,128)(2,1)} %acts.1, bf16[1024,512]{1,0:T(8,128)(2,1)} %w_query.1, bf16[1024,512]{1,0:T(8,128)(2,1)} %w_key.1, bf16[1024,512]{1,0:T(8,128)(2,1)} %w_value.1), custom_call_target="tpu_custom_call" | custom-call | flops 6039797760 | bytes 6291456 | tf_op jit(solution)/shard_map/pallas_call | solution.py:258
  126.7 1.8 %copy.6 = bf16[384,512]{1,0:T(8,128)(2,1)} copy(bf16[384,512]{1,0:T(8,128)(2,1)} %shard_map.46) | data formatting | bytes 786432

commit v6 on v3

--- a/solution.py
+++ b/solution.py
@@ -166,18 +166,18 @@
         for k in range(CHUNKS):
             each_at(t, lambda b, side: pass_on(b, side, k))
             each_at(t - 1, lambda b, side: across(b, k))
-            if t == 1 and 1 <= k <= 3:
+            if t == 2 and 1 <= k <= 3:
                 for j in range(1, n):
                     w_arrival(j, k - 1).wait_recv()
                     y_copy(j, k - 1).start()
-            if t == n - 1 and k == 0:
+            if t == n - 1 and k == 3:
                 for copy in own_copies:
                     copy.wait()
                 for j in range(1, n):
                     for i in range(3):
                         y_arrival(j, i).wait_recv()
-            if t == n - 1 and k < n - 2:
-                project(k)
+            if t == n - 1 and k >= 3 and k - 3 < n - 2:
+                project(k - 3)
     project(n - 2)
 
     @pl.loop(0, CHUNKS)

time: 109 us -> 112 us (1.028)
  Pallas kernels: 107 us -> 110 us
    pallas_call x1, Pallas kernels: 107 us -> 110 us  [one_head_per_device(): pl.pallas_call(functools.partial(head_kernel, n), out_shape=jax.ShapeDtyp...]
where the time goes in v6:
time: 112 us
  Pallas kernels  110 us (98%)
  local copies, waits for them, and re-layouts  1.77 us (2%)
    pallas_call x1, Pallas kernels, one_head_per_device(): pl.pallas_call(functools.partial(head_kernel, n), out_shape=jax.ShapeDtyp...  110 us

profile of v6, /device:TPU:0, one launch (start us, length us, event | category | flops | bytes accessed | tf_op | source)
XLA Modules:
  0.0 111.8 jit_solution(15166663183982246288)
XLA Ops:
  0.0 110.0 %shard_map.46 = bf16[384,512]{1,0:T(8,128)(2,1)} custom-call(bf16[192,2048]{1,0:T(8,128)(2,1)} %acts.1, bf16[1024,512]{1,0:T(8,128)(2,1)} %w_query.1, bf16[1024,512]{1,0:T(8,128)(2,1)} %w_key.1, bf16[1024,512]{1,0:T(8,128)(2,1)} %w_value.1), custom_call_target="tpu_custom_call" | custom-call | flops 6039797760 | bytes 6291456 | tf_op jit(solution)/shard_map/pallas_call | solution.py:251
  110.0 1.8 %copy.6 = bf16[384,512]{1,0:T(8,128)(2,1)} copy(bf16[384,512]{1,0:T(8,128)(2,1)} %shard_map.46) | data formatting | bytes 786432

commit v7 on v3

--- a/solution.py
+++ b/solution.py
@@ -99,14 +99,6 @@
 
     @pl.loop(0, CHUNKS)
     def _(k):
-        @pl.when(s < n - 1)
-        def _():
-            up_copy(s, k, True).start()
-
-        @pl.when(s > 0)
-        def _():
-            down_copy(s, k, True).start()
-
         x_copy(s, k, True).start()
         c_copy(s, k, r, True).start()
 
@@ -124,6 +116,20 @@
     ]
     for copy in own_copies:
         copy.start()
+
+    for i in range(2):
+        for j in range(1, n):
+            w_copy(j, i).wait_send()
+
+    @pl.loop(0, CHUNKS)
+    def _(k):
+        pl.when(s < n - 1)(lambda: up_copy(s, k, True).start())
+        pl.when(s > 0)(lambda: down_copy(s, k, True).start())
+
+    def weights_on(i):
+        for j in range(1, n):
+            w_arrival(j, i).wait_recv()
+            y_copy(j, i).start()
 
     def each_at(t, body):
         if t == 0:
@@ -162,14 +168,14 @@
                 total += jnp.dot(x_all[b, 1], w_all[half_width:, :], preferred_element_type=jnp.float32)
                 qkv[pl.ds(pl.multiple_of(b * block, block), block), :] = total.astype(jnp.bfloat16)
 
+    weights_on(0)
+    weights_on(1)
     for t in range(1, n):
         for k in range(CHUNKS):
             each_at(t, lambda b, side: pass_on(b, side, k))
             each_at(t - 1, lambda b, side: across(b, k))
-            if t == 1 and 1 <= k <= 3:
-                for j in range(1, n):
-                    w_arrival(j, k - 1).wait_recv()
-                    y_copy(j, k - 1).start()
+            if t == 1 and k == 1:
+                weights_on(2)
             if t == n - 1 and k == 0:
                 for copy in own_copies:
                     copy.wait()
@@ -221,8 +227,8 @@
     own_out.start()
 
     for j in range(1, n):
+        w_copy(j, 2).wait_send()
         for i in range(3):
-            w_copy(j, i).wait_send()
             y_copy(j, i).wait_send()
 
     @pl.loop(0, n)

time: 109 us -> 111 us (1.018)
  Pallas kernels: 107 us -> 109 us
    pallas_call x1, Pallas kernels: 107 us -> 109 us  [one_head_per_device(): pl.pallas_call(functools.partial(head_kernel, n), out_shape=jax.ShapeDtyp...]
where the time goes in v7:
time: 111 us
  Pallas kernels  109 us (98%)
  local copies, waits for them, and re-layouts  1.77 us (2%)
    pallas_call x1, Pallas kernels, one_head_per_device(): pl.pallas_call(functools.partial(head_kernel, n), out_shape=jax.ShapeDtyp...  109 us

profile of v7, /device:TPU:0, one launch (start us, length us, event | category | flops | bytes accessed | tf_op | source)
XLA Modules:
  0.0 110.8 jit_solution(18304314134364532365)
XLA Ops:
  0.0 109.0 %shard_map.46 = bf16[384,512]{1,0:T(8,128)(2,1)} custom-call(bf16[192,2048]{1,0:T(8,128)(2,1)} %acts.1, bf16[1024,512]{1,0:T(8,128)(2,1)} %w_query.1, bf16[1024,512]{1,0:T(8,128)(2,1)} %w_key.1, bf16[1024,512]{1,0:T(8,128)(2,1)} %w_value.1), custom_call_target="tpu_custom_call" | custom-call | flops 6039797760 | bytes 6291456 | tf_op jit(solution)/shard_map/pallas_call | solution.py:257
  109.0 1.8 %copy.6 = bf16[384,512]{1,0:T(8,128)(2,1)} copy(bf16[384,512]{1,0:T(8,128)(2,1)} %shard_map.46) | data formatting | bytes 786432

commit v8 on v3

--- a/solution.py
+++ b/solution.py
@@ -11,13 +11,14 @@
 HD = 128
 SPAN = 4
 CHUNKS = 6
+PIECES = 4
 MESH = pl.DeviceIdType.MESH
 
 
 def head_kernel(
     n, acts, w_query, w_key, w_value, out,
-    x_all, w_all, qkv, heads_out,
-    local_sem, w_send, w_recv, y_send, y_recv,
+    x_all, w_all, packed, qkv, heads_out,
+    local_sem, pack_sem, w_send, w_recv, y_send, y_recv,
     up_send, down_send, z_recv, x_send, x_recv, c_send, c_recv, o_send, o_recv,
 ):
     g, s = lax.axis_index("groups"), lax.axis_index("seq")
@@ -26,6 +27,7 @@
     rows, half_width = acts.shape
     depth = w_query.shape[0]
     half = depth // 2
+    piece = half // PIECES
     block = 2 * rows
     part = rows // CHUNKS
 
@@ -42,29 +44,32 @@
             src_ref=src, dst_ref=dst, send_sem=send, recv_sem=recv, device_id=device, device_id_type=MESH
         )
 
-    def w_rows(owner, which):
-        return pl.ds(pl.multiple_of(owner * depth + which * half, half), half)
-
-    def w_copy(j, i):
+    def w_rows(owner, which, q):
+        return pl.ds(pl.multiple_of(owner * depth + which * half + q * piece, piece), piece)
+
+    def w_pack(j, i):
         dest = lax.rem(s + j, n)
+        return pltpu.make_async_copy(
+            weights[i].at[pl.ds(pl.multiple_of(g * half, half), half), pl.ds(pl.multiple_of(dest * HD, HD), HD)],
+            packed.at[j - 1, :, pl.ds(i * HD, HD)], pack_sem.at[j - 1, i],
+        )
+
+    def w_copy(j, q):
         return remote(
-            weights[i].at[pl.ds(pl.multiple_of(g * half, half), half), pl.ds(pl.multiple_of(dest * HD, HD), HD)],
-            w_all.at[w_rows(s, g), pl.ds(i * HD, HD)],
-            w_send.at[j - 1, i], w_recv.at[j - 1, i], seq=dest,
-        )
-
-    def w_arrival(j, i):
-        owner = lax.rem(s + n - j, n)
-        here = w_all.at[w_rows(owner, g), pl.ds(i * HD, HD)]
-        return remote(here, here, w_send.at[j - 1, i], w_recv.at[j - 1, i], seq=lax.rem(s + j, n))
-
-    def y_copy(j, i, which=g):
-        owner = lax.rem(s + n - j, n)
-        here = w_all.at[w_rows(owner, which), pl.ds(i * HD, HD)]
-        return remote(here, here, y_send.at[j - 1, i], y_recv.at[j - 1, i], groups=1 - g)
-
-    def y_arrival(j, i):
-        return y_copy(j, i, 1 - g)
+            packed.at[j - 1, pl.ds(q * piece, piece), :], w_all.at[w_rows(s, g, q), :],
+            w_send.at[j - 1, q], w_recv.at[j - 1, q], seq=lax.rem(s + j, n),
+        )
+
+    def w_arrival(j, q):
+        here = w_all.at[w_rows(lax.rem(s + n - j, n), g, q), :]
+        return remote(here, here, w_send.at[j - 1, q], w_recv.at[j - 1, q], seq=lax.rem(s + j, n))
+
+    def y_copy(j, q, which=g):
+        here = w_all.at[w_rows(lax.rem(s + n - j, n), which, q), :]
+        return remote(here, here, y_send.at[j - 1, q], y_recv.at[j - 1, q], groups=1 - g)
+
+    def y_arrival(j, q):
+        return y_copy(j, q, 1 - g)
 
     def spot(b, rr, cc, k):
         return x_all.at[b, cc, pl.ds(pl.multiple_of(rr * rows + k * part, part), part), :]
@@ -93,9 +98,14 @@
         here = spot(b, rr, 1 - c, k)
         return remote(here, here, c_send.at[rr, b, k], c_recv.at[rr, b, k], col=1 - c)
 
-    for i in range(3):
-        for j in range(1, n):
-            w_copy(j, i).start()
+    for j in range(1, n):
+        for i in range(3):
+            w_pack(j, i).start()
+    for j in range(1, n):
+        for i in range(3):
+            w_pack(j, i).wait()
+        for q in range(PIECES):
+            w_copy(j, q).start()
 
     @pl.loop(0, CHUNKS)
     def _(k):
@@ -166,7 +176,7 @@
         for k in range(CHUNKS):
             each_at(t, lambda b, side: pass_on(b, side, k))
             each_at(t - 1, lambda b, side: across(b, k))
-            if t == 1 and 1 <= k <= 3:
+            if t == 1 and 1 <= k <= PIECES:
                 for j in range(1, n):
                     w_arrival(j, k - 1).wait_recv()
                     y_copy(j, k - 1).start()
@@ -174,8 +184,8 @@
                 for copy in own_copies:
                     copy.wait()
                 for j in range(1, n):
-                    for i in range(3):
-                        y_arrival(j, i).wait_recv()
+                    for q in range(PIECES):
+                        y_arrival(j, q).wait_recv()
             if t == n - 1 and k < n - 2:
                 project(k)
     project(n - 2)
@@ -221,9 +231,9 @@
     own_out.start()
 
     for j in range(1, n):
-        for i in range(3):
-            w_copy(j, i).wait_send()
-            y_copy(j, i).wait_send()
+        for q in range(PIECES):
+            w_copy(j, q).wait_send()
+            y_copy(j, q).wait_send()
 
     @pl.loop(0, n)
     def _(b):
@@ -256,10 +266,11 @@
         scratch_shapes=[
             pltpu.VMEM((n, 2, 2 * rows, half_width), jnp.bfloat16),
             pltpu.VMEM((n * depth, 3 * HD), jnp.bfloat16),
+            pltpu.VMEM((n - 1, depth // 2, 3 * HD), jnp.bfloat16),
             pltpu.VMEM((tokens, 3 * HD), jnp.bfloat16),
             pltpu.VMEM((n, 2 * rows, HD), jnp.bfloat16),
-            dma((4,)),
-            dma((n - 1, 3)), dma((n - 1, 3)), dma((n - 1, 3)), dma((n - 1, 3)),
+            dma((4,)), dma((n - 1, 3)),
+            dma((n - 1, PIECES)), dma((n - 1, PIECES)), dma((n - 1, PIECES)), dma((n - 1, PIECES)),
             dma((n, CHUNKS)), dma((n, CHUNKS)), dma((n, CHUNKS)),
             dma((n, CHUNKS)), dma((n, CHUNKS)),
             dma((2, n, CHUNKS)), dma((2, n, CHUNKS)),
@@ -329,7 +340,7 @@
     n = lax.axis_size("seq")
     pairs = all(lax.axis_size(axis) == 2 for axis in ("groups", "row", "col"))
     depth, width = w_query.shape
-    if pairs and n == SPAN and width == n * HD and acts.shape[0] % (16 * CHUNKS) == 0 and depth % 32 == 0:
+    if pairs and n == SPAN and width == n * HD and acts.shape[0] % (16 * CHUNKS) == 0 and depth % (32 * PIECES) == 0:
         return one_head_per_device(acts, w_query, w_key, w_value)
     return blocks_passed_along(acts, w_query, w_key, w_value)
 

time: 109 us -> 110 us (level)
  no operation moved by 1% of the time
where the time goes in v8:
time: 110 us
  Pallas kernels  108 us (98%)
  local copies, waits for them, and re-layouts  1.77 us (2%)
    pallas_call x1, Pallas kernels, one_head_per_device(): pl.pallas_call(functools.partial(head_kernel, n), out_shape=jax.ShapeDtyp...  108 us

profile of v8, /device:TPU:0, one launch (start us, length us, event | category | flops | bytes accessed | tf_op | source)
XLA Modules:
  0.0 109.8 jit_solution(3206838212584335551)
XLA Ops:
  0.0 108.1 %shard_map.46 = bf16[384,512]{1,0:T(8,128)(2,1)} custom-call(bf16[192,2048]{1,0:T(8,128)(2,1)} %acts.1, bf16[1024,512]{1,0:T(8,128)(2,1)} %w_query.1, bf16[1024,512]{1,0:T(8,128)(2,1)} %w_key.1, bf16[1024,512]{1,0:T(8,128)(2,1)} %w_value.1), custom_call_target="tpu_custom_call" | custom-call | flops 6039797760 | bytes 6291456 | tf_op jit(solution)/shard_map/pallas_call | solution.py:261
  108.1 1.8 %copy.6 = bf16[384,512]{1,0:T(8,128)(2,1)} copy(bf16[384,512]{1,0:T(8,128)(2,1)} %shard_map.46) | data formatting | bytes 786432

commit v9 on v4

--- a/solution.py
+++ b/solution.py
@@ -187,7 +187,7 @@
             tops[b] = top
             totals[b], sums[b] = weigh(scores, top, qkv[near, pl.ds(2 * HD, HD)])
 
-    for t in range(1, n - 1):
+    for t in range(1, n):
         for k in range(CHUNKS):
             each_at(t, lambda b, side: pass_on(b, side, k))
             each_at(t - 1, lambda b, side: across(b, k))
@@ -195,29 +195,20 @@
                 for j in range(1, n):
                     w_arrival(j, k - 1).wait_recv()
                     y_copy(j, k - 1).start()
+            if t == n - 1 and k == 0:
+                for copy in own_copies:
+                    copy.wait()
+                for j in range(1, n):
+                    for i in range(3):
+                        y_arrival(j, i).wait_recv()
+            if t == n - 1 and k < n - 2:
+                project(k)
+    project(n - 2)
 
     for k in range(CHUNKS):
-        each_at(n - 1, lambda b, side: pass_on(b, side, k))
-        if k == 0:
-            for copy in own_copies:
-                copy.wait()
-            for j in range(1, n):
-                for i in range(3):
-                    y_arrival(j, i).wait_recv()
-        if k < 2:
-            @pl.loop(k * (CHUNKS // 2), (k + 1) * (CHUNKS // 2))
-            def _(kk):
-                each_at(n - 2, lambda b, side: across(b, kk))
-        if k < n - 1:
-            project(k)
-        if k == 3:
-            pl.loop(0, 2)(attend_near)
-        if k == 4:
-            attend_near(2)
-
-    @pl.loop(0, CHUNKS)
-    def _(k):
         each_at(n - 1, lambda b, side: across(b, k))
+        if CHUNKS - n <= k < CHUNKS - 1:
+            attend_near(k - (CHUNKS - n))
 
     project(n - 1)
 

time: 112 us -> 109 us (0.973)
  Pallas kernels: 110 us -> 107 us
    pallas_call x1, Pallas kernels: 110 us -> 107 us  [one_head_per_device(): pl.pallas_call(functools.partial(head_kernel, n), out_shape=jax.ShapeDtyp...]
where the time goes in v9:
time: 109 us
  Pallas kernels  107 us (98%)
  local copies, waits for them, and re-layouts  1.77 us (2%)
    pallas_call x1, Pallas kernels, one_head_per_device(): pl.pallas_call(functools.partial(head_kernel, n), out_shape=jax.ShapeDtyp...  107 us

profile of v9, /device:TPU:0, one launch (start us, length us, event | category | flops | bytes accessed | tf_op | source)
XLA Modules:
  0.0 108.8 jit_solution(6821637358115737537)
XLA Ops:
  0.0 107.0 %shard_map.46 = bf16[384,512]{1,0:T(8,128)(2,1)} custom-call(bf16[192,2048]{1,0:T(8,128)(2,1)} %acts.1, bf16[1024,512]{1,0:T(8,128)(2,1)} %w_query.1, bf16[1024,512]{1,0:T(8,128)(2,1)} %w_key.1, bf16[1024,512]{1,0:T(8,128)(2,1)} %w_value.1), custom_call_target="tpu_custom_call" | custom-call | flops 6039797760 | bytes 6291456 | tf_op jit(solution)/shard_map/pallas_call | solution.py:283
  107.0 1.8 %copy.6 = bf16[384,512]{1,0:T(8,128)(2,1)} copy(bf16[384,512]{1,0:T(8,128)(2,1)} %shard_map.46) | data formatting | bytes 786432
